TPU v7x, 128 devices: a whole 4x4x4 slice. The times are simulated.
128 devices in a mesh: seq: 16 (over z, y), expert: 8 (over x, core).
Axes of the slice: x: 4, y: 4, z: 4, core: 2. Of those that a mesh axis runs over, the one named last changes fastest.
Arguments:
- tokens: bfloat16 [2048, 4096], P(('seq', 'expert')), may hold values from -6 to 6
- gain_mamba: float32 [4096], replicated, may hold values from 0.1 to 1.9
- in_weight: bfloat16 [2, 4096, 8192], P(None, 'seq', 'expert'), may hold values from -0.09375 to 0.09375
- conv_weight: float32 [4, 8192], P(None, 'expert'), may hold values from -3 to 3
- conv_bias: float32 [8192], P('expert'), may hold values from -3 to 3
- xproj_weight: bfloat16 [8192, 288], P('expert'), may hold values from -0.0625 to 0.0625
- dt_weight: bfloat16 [256, 8192], P(None, 'expert'), may hold values from -0.375 to 0.375
- dt_bias: float32 [8192], P('expert'), may hold values from -7 to -2
- a_rate: float32 [16, 8192], P(None, 'expert'), may hold values from 0.01 to 8
- skip_d: float32 [8192], P('expert'), may hold values from 0.5 to 1.5
- out_weight: bfloat16 [8192, 4096], P('expert', 'seq'), may hold values from -0.0625 to 0.0625
- gain_moe: float32 [4096], replicated, may hold values from 0.1 to 1.9
- expert_ids: int32 [2048, 2], P(('seq', 'expert')), may hold values from 0 to 15, all different within a row; in each aligned block of 16 rows (0 to 15, 16 to 31, ...) at most 4 rows name the same one
- gate_weights: float32 [2048, 2], P(('seq', 'expert')), may hold values from 0.2 to 1
- w_gate: bfloat16 [16, 4096, 7168], P('seq', None, 'expert'), may hold values from -0.09375 to 0.09375
- w_up: bfloat16 [16, 4096, 7168], P('seq', None, 'expert'), may hold values from -0.09375 to 0.09375
- w_down: bfloat16 [16, 7168, 4096], P('seq', 'expert'), may hold values from -0.0625 to 0.0625
Outputs:
- mixed: bfloat16 [2048, 4096], P(('seq', 'expert'))
Inputs may be any that keep to these rules, and one draw needn't show every extreme that they name: `expert_ids`: each row names 2 different experts. In each aligned block of 16 rows (the rows of one device) no expert is named by more than 4 rows, a bound that some block reaches.
All inputs are finite; a program needn't handle non-finite values.
Results may differ from a plain program's by a relative error of at most 0.03.
Values may be sent and summed in bfloat16 or wider, within the bound.
A program may use at most 192 MiB of HBM per device.

v0:
```python
import jax
import jax.numpy as jnp
from jax import lax
from jax.sharding import PartitionSpec as P

STATE = 16
CONV = 4
RANK = 256
TOP = 2


def from_behind(block, axis, distance):
    devices = range(lax.axis_size(axis))
    route = [(i - distance, i) for i in devices if i - distance in devices]
    return lax.ppermute(block, axis, route)


def rms_norm(values, gain):
    wide = values.astype(jnp.float32)
    return wide * lax.rsqrt(jnp.mean(wide * wide, axis=-1, keepdims=True) + 1e-05) * gain


def combine_states(earlier, later):
    return (earlier[0] * later[0], later[0] * earlier[1] + later[1])


def per_device(
    tokens,
    gain_mamba,
    in_weight,
    conv_weight,
    conv_bias,
    xproj_weight,
    dt_weight,
    dt_bias,
    a_rate,
    skip_d,
    out_weight,
    gain_moe,
    expert_ids,
    gate_weights,
    w_gate,
    w_up,
    w_down,
):
    rows, dim = tokens.shape
    n_seq = lax.axis_size("seq")
    n_exp = lax.axis_size("expert")
    group = lax.all_gather(tokens, "expert", axis=0, tiled=True)
    local_tok = group.shape[0]
    normed = rms_norm(group, gain_mamba).astype(jnp.bfloat16)
    both = jnp.einsum(
        "td,kdc->tkc",
        normed,
        lax.all_gather(in_weight, "seq", axis=1, tiled=True),
        preferred_element_type=jnp.float32,
    )
    xpart = both[:, 0]
    zpart = both[:, 1]
    edge = from_behind(xpart[local_tok - (CONV - 1) :], "seq", 1)
    padded = jnp.concatenate([edge, xpart], axis=0)
    conv = conv_bias
    for tap in range(CONV):
        conv = conv + conv_weight[tap] * padded[tap : tap + local_tok]
    inner = jax.nn.silu(conv).astype(jnp.bfloat16)
    partial_value = jnp.dot(inner, xproj_weight, preferred_element_type=jnp.float32)
    low_part, edge_part = (
        lax.psum(partial_value[:, :RANK].astype(jnp.bfloat16), "expert").astype(jnp.float32),
        lax.psum(partial_value[:, RANK:].astype(jnp.bfloat16), "expert").astype(jnp.float32),
    )
    dt_low = low_part.astype(jnp.bfloat16)
    bmat = edge_part[:, :STATE]
    cmat = edge_part[:, STATE:]
    step = jax.nn.softplus(jnp.dot(dt_low, dt_weight, preferred_element_type=jnp.float32) + dt_bias)
    inner_f = inner.astype(jnp.float32)
    decay = jnp.exp(-step[:, None, :] * a_rate[None, :, :])
    source = bmat[:, :, None] * (step * inner_f)[:, None, :]
    cumulative, states = lax.associative_scan(combine_states, (decay, source), axis=0)
    total = cumulative[-1]
    final = states[-1]

    def relay(turn, incoming):
        return from_behind((total * incoming + final).astype(jnp.bfloat16), "seq", 1).astype(
            jnp.float32
        )

    arriving = lax.fori_loop(0, n_seq - 1, relay, jnp.zeros_like(final))
    states = states + cumulative * arriving[None, :, :]
    readout = jnp.sum(cmat[:, :, None] * states, axis=1)
    gated = ((readout + skip_d * inner_f) * jax.nn.silu(zpart)).astype(jnp.bfloat16)
    terms = jnp.dot(
        gated,
        lax.all_gather(out_weight, "seq", axis=1, tiled=True),
        preferred_element_type=jnp.float32,
    )
    mixer = lax.psum_scatter(
        terms.astype(jnp.bfloat16), "expert", scatter_dimension=0, tiled=True
    ).astype(jnp.float32)
    resid = (tokens.astype(jnp.float32) + mixer).astype(jnp.bfloat16)
    normed2 = rms_norm(resid, gain_moe).astype(jnp.bfloat16)
    capacity = max(2, 4 * rows // n_seq)
    slots_all = n_seq * capacity
    flat_ids = expert_ids.reshape(-1)
    onehot = (flat_ids[:, None] == jnp.arange(n_seq, dtype=jnp.int32)[None, :]).astype(jnp.int32)
    before = jnp.cumsum(onehot, axis=0) - onehot
    slot = jnp.sum(before * onehot, axis=1)
    target = flat_ids * capacity + slot
    places = target[:, None] == jnp.arange(slots_all, dtype=jnp.int32)[None, :]
    dispatch_mat = jnp.any(places.reshape(rows, TOP, slots_all), axis=1).astype(jnp.bfloat16)
    send = jnp.einsum(
        "rp,rd->pd", dispatch_mat, normed2, preferred_element_type=jnp.float32
    ).astype(jnp.bfloat16)
    received = lax.all_to_all(
        send.reshape(n_seq, capacity, dim), "seq", split_axis=0, concat_axis=0, tiled=True
    )
    pooled = lax.all_gather(
        received.reshape(1, slots_all, dim), "expert", axis=0, tiled=True
    ).reshape(n_exp * slots_all, dim)
    gate = jnp.dot(pooled, w_gate[0], preferred_element_type=jnp.float32)
    upper = jnp.dot(pooled, w_up[0], preferred_element_type=jnp.float32)
    act = (jax.nn.silu(gate) * upper).astype(jnp.bfloat16)
    outputs = lax.psum_scatter(
        jnp.dot(act, w_down[0], preferred_element_type=jnp.float32).astype(jnp.bfloat16),
        "expert",
        scatter_dimension=0,
        tiled=True,
    )
    returned = lax.all_to_all(
        outputs.reshape(n_seq, capacity, dim), "seq", split_axis=0, concat_axis=0, tiled=True
    ).reshape(slots_all, dim)
    weighting = jnp.where(places, gate_weights.reshape(-1)[:, None], 0.0)
    weighting = jnp.sum(weighting.reshape(rows, TOP, slots_all), axis=1)
    moe = jnp.dot(weighting, returned.astype(jnp.float32), precision=lax.Precision.HIGHEST)
    return (resid.astype(jnp.float32) + moe).astype(jnp.bfloat16)


def solution(mesh):
    placed = (
        P(("seq", "expert"), None),
        P(),
        P(None, "seq", "expert"),
        P(None, "expert"),
        P("expert"),
        P("expert", None),
        P(None, "expert"),
        P("expert"),
        P(None, "expert"),
        P("expert"),
        P("expert", "seq"),
        P(),
        P(("seq", "expert"), None),
        P(("seq", "expert"), None),
        P("seq", None, "expert"),
        P("seq", None, "expert"),
        P("seq", "expert", None),
    )
    return jax.shard_map(
        per_device,
        mesh=mesh,
        in_specs=placed,
        out_specs=P(("seq", "expert"), None),
        check_vma=False,
    )
```

profile of v0, /device:TPU:0, one launch (start us, length us, event | category | flops | bytes accessed | tf_op | source)
XLA Modules:
  0.0 908.5 jit_solution(7577490913799089768)
XLA Ops:
  8.9 26.0 %all-gather.5.cloned.1.call-done = bf16[128,4096]{1,0:T(8,128)(2,1)} async-done(((bf16[16,4096]{1,0:T(8,128)(2,1)}), bf16[128,4096]{1,0:T(8,128)(2,1)}) %all-gather.5.cloned.1.call-update) | async-done | bytes 1048592 | tf_op jit(solution)/shard_map/all_gather | solution.py:49
  36.5 111.9 %all-gather.7.cloned.1.call-done = bf16[2,4096,1024]{2,1,0:T(8,128)(2,1)} async-done(((bf16[2,256,1024]{2,1,0:T(8,128)(2,1)}), bf16[2,4096,1024]{2,1,0:T(8,128)(2,1)}) %all-gather.7.cloned.1.call-update) | async-done | bytes 16777232 | tf_op jit(solution)/shard_map/all_gather | solution.py:55
  148.4 8.5 fusion.20
  163.9 14.0 %psum.14 = bf16[128,32]{0,1:T(8,128)(2,1)S(1)} all-reduce(bf16[128,32]{0,1:T(8,128)(2,1)S(1)} %slice.341), channel_id=1, replica_groups=mesh['seq'=16,'expert'=8] {'expert'}, use_global_device_ids=true, to_apply=%region_1.2 | all-reduce | flops 4096 | bytes 16384 | tf_op jit(solution)/shard_map/psum | solution.py:69
  178.7 44.8 %all-reduce.30.cloned.1.call-done = bf16[128,256]{0,1:T(8,128)(2,1)} async-done(((bf16[128,256]{0,1:T(8,128)(2,1)}), bf16[128,256]{0,1:T(8,128)(2,1)}) %all-reduce.30.cloned.1.call-update) | async-done | bytes 65552 | tf_op jit(solution)/shard_map/psum | solution.py:68
  233.5 10.9 %slice_add_fusion = (f32[64,16,1024]{2,1,0:T(8,128)S(1)}, f32[64,16,1024]{2,1,0:T(8,128)}) fusion(f32[128,16,1024]{2,1,0:T(8,128)} %copy-done.3, f32[128,16,1024]{2,1,0:T(8,128)} %copy-done.2), kind=kLoop, calls=%fused_computation.19 | loop fusion | flops 3145728 | bytes 25165824 | tf_op jit(solution)/shard_map/add | solution.py:24
  308.4 7.0 pad.108
  315.3 10.2 %pad.109 = f32[32,16,1024]{2,1,0:T(8,128)} pad(f32[16,16,1024]{2,1,0:T(8,128)} %add.263, f32[]{:T(128)} %constant.13.clone.1), padding=1_0_1x0_0_0x0_0_0 | pad | bytes 3145732 | tf_op jit(solution)/shard_map/pad | solution.py:78
  325.5 10.1 %pad.95 = f32[32,16,1024]{2,1,0:T(8,128)} pad(f32[16,16,1024]{2,1,0:T(8,128)} %add.253, f32[]{:T(128)} %constant.13.clone.1), padding=1_0_1x0_0_0x0_0_0 | pad | bytes 3145732 | tf_op jit(solution)/shard_map/pad | solution.py:78
  337.9 10.2 %pad.94 = f32[32,16,1024]{2,1,0:T(8,128)} pad(f32[16,16,1024]{2,1,0:T(8,128)} %pad_maximum_fusion.4, f32[]{:T(128)} %constant.13.clone.1), padding=0_1_1x0_0_0x0_0_0 | pad | bytes 3145732 | tf_op jit(solution)/shard_map/pad | solution.py:78
  348.1 4.3 add.255
  355.3 5.0 fusion.16
  362.0 18.6 %pad.96 = f32[64,16,1024]{2,1,0:T(8,128)} pad(f32[32,16,1024]{2,1,0:T(8,128)} %pad_maximum_fusion.2, f32[]{:T(128)} %constant.13.clone.1), padding=0_1_1x0_0_0x0_0_0 | pad | bytes 6291460 | tf_op jit(solution)/shard_map/pad | solution.py:78
  380.6 12.0 %pad.97 = f32[64,16,1024]{2,1,0:T(8,128)} pad(f32[32,16,1024]{2,1,0:T(8,128)S(1)} %copy-done.16, f32[]{:T(128)} %constant.13.clone.1), padding=1_0_1x0_0_0x0_0_0 | pad | bytes 6291460 | tf_op jit(solution)/shard_map/pad | solution.py:78
  392.5 6.8 add.257
  399.4 35.6 %pad.99 = f32[128,16,1024]{2,1,0:T(8,128)} pad(f32[64,16,1024]{2,1,0:T(8,128)} %add.257, f32[]{:T(128)} %constant.13.clone.1), padding=1_0_1x0_0_0x0_0_0 | pad | bytes 12582916 | tf_op jit(solution)/shard_map/pad | solution.py:78
  436.5 18.6 %pad.110 = f32[64,16,1024]{2,1,0:T(8,128)} pad(f32[32,16,1024]{2,1,0:T(8,128)} %pad_maximum_fusion.3, f32[]{:T(128)} %constant.13.clone.1), padding=0_1_1x0_0_0x0_0_0 | pad | bytes 6291460 | tf_op jit(solution)/shard_map/pad | solution.py:78
  455.1 11.9 %pad.111 = f32[64,16,1024]{2,1,0:T(8,128)} pad(f32[32,16,1024]{2,1,0:T(8,128)S(1)} %copy-done.15, f32[]{:T(128)} %constant.13.clone.1), padding=1_0_1x0_0_0x0_0_0 | pad | bytes 6291460 | tf_op jit(solution)/shard_map/pad | solution.py:78
  467.0 7.1 add.265
  475.6 7.6 fusion.12
  485.7 35.5 %pad.98 = f32[128,16,1024]{2,1,0:T(8,128)} pad(f32[64,16,1024]{2,1,0:T(8,128)} %pad_maximum_fusion, f32[]{:T(128)} %constant.13.clone.1), padding=0_1_1x0_0_0x0_0_0 | pad | bytes 12582916 | tf_op jit(solution)/shard_map/pad | solution.py:78
  521.2 35.5 %pad.113 = f32[128,16,1024]{2,1,0:T(8,128)} pad(f32[64,16,1024]{2,1,0:T(8,128)} %add.265, f32[]{:T(128)} %constant.13.clone.1), padding=1_0_1x0_0_0x0_0_0 | pad | bytes 12582916 | tf_op jit(solution)/shard_map/pad | solution.py:78
  556.8 4.8 pad_maximum_fusion.1
  561.5 35.5 %pad.112 = f32[128,16,1024]{2,1,0:T(8,128)} pad(f32[64,16,1024]{2,1,0:T(8,128)} %pad_maximum_fusion.1, f32[]{:T(128)} %constant.13.clone.1), padding=0_1_1x0_0_0x0_0_0 | pad | bytes 12582916 | tf_op jit(solution)/shard_map/pad | solution.py:78
  598.8 107.7 %while.11 = (s32[]{:T(128)}, f32[16,1024]{1,0:T(8,128)S(1)}, f32[16,1024]{1,0:T(8,128)S(1)}, f32[16,1024]{1,0:T(8,128)S(1)}, s32[]{:T(128)}, /*index=5*/s32[]{:T(128)}) while((s32[]{:T(128)}, f32[16,1024]{1,0:T(8,128)S(1)}, f32[16,1024]{1,0:T(8,128)S(1)}, f32[16,1024]{1,0:T(8,128)S(1)}, s32[]{:T(128)}, /*index=5*/s32[]{:T(128)}) %tuple.47), condition=%wide.region_4.5_spmd.clone, body=%wide.region_3.4_spmd.clone.sunk | while | flops 81923 | bytes 458871 | solution.py:87
  603.9 4.2 collective-permute-start
  609.7 4.3 collective-permute-start
  621.5 4.2 collective-permute-start
  627.3 5.6 collective-permute-start
  634.5 6.5 collective-permute-start
  642.6 6.5 collective-permute-start
  650.7 6.3 collective-permute-start
  658.6 6.3 collective-permute-start
  666.6 6.3 collective-permute-start
  674.6 6.2 collective-permute-start
  682.5 6.3 collective-permute-start
  690.4 6.5 collective-permute-start
  698.5 6.3 collective-permute-start
  706.5 14.0 %multiply_reduce_fusion = f32[128,1024]{1,0:T(8,128)S(1)} fusion(f32[128,16,1024]{2,1,0:T(8,128)} %pad.112, f32[128,16,1024]{2,1,0:T(8,128)} %pad.113, f32[128,16,1024]{2,1,0:T(8,128)} %pad.98, f32[128,16,1024]{2,1,0:T(8,128)} %pad.99, f32[16,1024]{1,0:T(8,128)S(1)} %get-tuple-element.27, f32[128,16]{1,0:T(8,128)S(1)} %copy-done.28), kind=kLoop, calls=%fused_computation.3 | loop fusion | flops 12451840 | bytes 34152448 | tf_op jit(solution)/shard_map/reduce_sum | solution.py:89
  720.5 5.7 convolution_convert_fusion
  727.1 39.7 %reduce-scatter.3.cloned.1.call-done = bf16[16,4096]{1,0:T(8,128)(2,1)} async-done(((bf16[128,4096]{1,0:T(8,128)(2,1)}), bf16[16,4096]{1,0:T(8,128)(2,1)}) %reduce-scatter.3.cloned.1.call-update) | async-done | bytes 131088 | tf_op jit(solution)/shard_map/reduce_scatter | solution.py:96
  769.3 16.9 %all_to_all.10 = bf16[16,4,4096]{2,1,0:T(4,128)(2,1)S(1)} all-to-all(bf16[16,4,4096]{2,1,0:T(4,128)(2,1)S(1)} %reshape.78), channel_id=1, replica_groups=mesh['seq'=16,'expert'=8] {'seq'}, dimensions={0} | all-to-all | bytes 1048576 | tf_op jit(solution)/shard_map/all_to_all | solution.py:113
  787.2 29.3 %all-gather.11.cloned.1.call-done = bf16[8,64,4096]{2,1,0:T(8,128)(2,1)} async-done(((bf16[1,64,4096]{2,1,0:T(8,128)(2,1)}), bf16[8,64,4096]{2,1,0:T(8,128)(2,1)}) %all-gather.11.cloned.1.call-update) | async-done | bytes 4194320 | tf_op jit(solution)/shard_map/all_gather | solution.py:116
  816.5 10.1 %fusion.6 = f32[512,896]{1,0:T(8,128)} fusion(bf16[512,4096]{1,0:T(8,128)(2,1)} %bitcast.51, bf16[1,4096,896]{2,1,0:T(8,128)(2,1)} %param.33), kind=kOutput, calls=%fused_computation.9 | convolution fusion | flops 3758096384 | bytes 13369344 | tf_op jit(solution)/shard_map/dot_general | solution.py:119
  826.6 16.7 %fusion.8 = bf16[512,4096]{1,0:T(8,128)(2,1)} fusion(bf16[1,896,4096]{2,1,0:T(8,128)(2,1)} %param.35, f32[512,896]{1,0:T(8,128)} %fusion.6, bf16[512,4096]{1,0:T(8,128)(2,1)} %bitcast.52, bf16[1,4096,896]{2,1,0:T(8,128)(2,1)} %param.34), kind=kOutput, calls=%fused_computation.11 | convolution fusion | flops 7521042432 | bytes 24903680 | tf_op jit(solution)/shard_map/dot_general | solution.py:123
  843.3 38.0 %reduce-scatter.5.cloned.1.call-done = bf16[64,4096]{1,0:T(8,128)(2,1)} async-done(((bf16[512,4096]{1,0:T(8,128)(2,1)}), bf16[64,4096]{1,0:T(8,128)(2,1)}) %reduce-scatter.5.cloned.1.call-update) | async-done | bytes 524304 | tf_op jit(solution)/shard_map/reduce_scatter | solution.py:122
  883.3 7.1 all-to-all-start.1
  890.5 10.1 %all-to-all-done.1 = bf16[16,4,4096]{2,1,0:T(4,128)(2,1)S(1)} async-done(((bf16[16,4,4096]{2,1,0:T(4,128)(2,1)}), bf16[16,4,4096]{2,1,0:T(4,128)(2,1)S(1)}, u32[]{:S(2)}, u32[]{:S(2)}) %all-to-all-start.1) | async-done | bytes 524320 | tf_op jit(solution)/shard_map/all_to_all | solution.py:128
  (241 shorter events, 138.8 us)
Async XLA Ops:
  6.5 155.7 %copy-start = (bf16[1024,288]{0,1:T(8,128)(2,1)S(1)}, bf16[1024,288]{0,1:T(8,128)(2,1)}, u32[]{:S(2)}) copy-start(bf16[1024,288]{0,1:T(8,128)(2,1)} %param.24) | copy-start | bytes 1769476
  6.5 28.4 %all-gather.5.cloned.1.call-start = ((), (), s32[]{:S(2)}) async-start(), calls=%async_computation.4 | async-start | bytes 1179648 | tf_op jit(solution)/shard_map/all_gather | solution.py:49
  7.3 141.1 %all-gather.7.cloned.1.call-start = ((), (), s32[]{:S(2)}) async-start(), calls=%async_computation.5 | async-start | bytes 17825792 | tf_op jit(solution)/shard_map/all_gather | solution.py:55
  8.0 215.6 %all-reduce.30.cloned.1.call-start = ((), (), s32[]{:S(2)}) async-start(), calls=%async_computation.6 | async-start | bytes 131072 | tf_op jit(solution)/shard_map/psum | solution.py:68
  36.4 125.5 %copy-start.39 = (f32[1024]{0:T(1024)S(1)}, f32[1024]{0:T(1024)}, u32[]{:S(2)}) copy-start(f32[1024]{0:T(1024)} %param.23) | copy-start | bytes 12292
  36.4 187.1 %copy-start.42 = (bf16[256,1024]{1,0:T(8,128)(2,1)S(1)}, bf16[256,1024]{1,0:T(8,128)(2,1)}, u32[]{:S(2)}) copy-start(bf16[256,1024]{1,0:T(8,128)(2,1)} %param.25) | copy-start | bytes 1572868
  36.4 187.1 %copy-start.43 = (f32[1024]{0:T(1024)S(1)}, f32[1024]{0:T(1024)}, u32[]{:S(2)}) copy-start(f32[1024]{0:T(1024)} %param.26) | copy-start | bytes 12292
  156.9 68.0 %copy-start.37 = (f32[16,1024]{1,0:T(8,128)S(1)}, f32[16,1024]{1,0:T(8,128)}, u32[]{:S(2)}) copy-start(f32[16,1024]{1,0:T(8,128)} %param.27) | copy-start | bytes 196612
  156.9 5.0 collective-permute-start.1
  162.2 64.8 %copy-start.23 = (bf16[128,1024]{1,0:T(8,128)(2,1)}, bf16[128,1024]{1,0:T(8,128)(2,1)S(1)}, u32[]{:S(2)}) copy-start(bf16[128,1024]{1,0:T(8,128)(2,1)S(1)} %multiply_convert_fusion.1) | copy-start | bytes 786436
  163.2 557.3 %all-gather.9.cloned.1.call-start = ((), (), s32[]{:S(2)}) async-start(), calls=%async_computation.7 | async-start | bytes 8912896 | tf_op jit(solution)/shard_map/all_gather | solution.py:93
  163.8 602.9 %reduce-scatter.3.cloned.1.call-start = ((), (), s32[]{:S(2)}) async-start(), calls=%async_computation.8 | async-start | bytes 1179648 | tf_op jit(solution)/shard_map/reduce_scatter | solution.py:96
  280.3 8.2 copy-start.36
  288.5 8.3 copy-start.20
  308.4 27.3 %copy-start.33 = (f32[1,16,1024]{2,1,0:T(8,128)S(1)}, f32[1,16,1024]{2,1,0:T(8,128)}, u32[]{:S(2)}) copy-start(f32[1,16,1024]{2,1,0:T(8,128)} %slice.347) | copy-start | bytes 196612
  362.0 18.6 %copy-start.16 = (f32[32,16,1024]{2,1,0:T(8,128)S(1)}, f32[32,16,1024]{2,1,0:T(8,128)}, u32[]{:S(2)}) copy-start(f32[32,16,1024]{2,1,0:T(8,128)} %add.255) | copy-start | bytes 6291460
  399.4 35.6 %copy-start.17 = (f32[31,16,1024]{2,1,0:T(8,128)S(1)}, f32[31,16,1024]{2,1,0:T(8,128)}, u32[]{:S(2)}) copy-start(f32[31,16,1024]{2,1,0:T(8,128)} %get-tuple-element.56) | copy-start | bytes 6094852
  399.4 35.6 %copy-start.31 = (f32[1,16,1024]{2,1,0:T(8,128)S(1)}, f32[1,16,1024]{2,1,0:T(8,128)}, u32[]{:S(2)}) copy-start(f32[1,16,1024]{2,1,0:T(8,128)} %slice.369) | copy-start | bytes 196612
  436.5 18.6 %copy-start.15 = (f32[32,16,1024]{2,1,0:T(8,128)S(1)}, f32[32,16,1024]{2,1,0:T(8,128)}, u32[]{:S(2)}) copy-start(f32[32,16,1024]{2,1,0:T(8,128)} %add.264) | copy-start | bytes 6291460
  467.0 8.6 copy-start.6
  521.2 35.5 %copy-start.29 = (f32[1,16,1024]{2,1,0:T(8,128)S(1)}, f32[1,16,1024]{2,1,0:T(8,128)}, u32[]{:S(2)}) copy-start(f32[1,16,1024]{2,1,0:T(8,128)} %slice.368) | copy-start | bytes 196612
  561.5 144.9 %copy-start.28 = (f32[128,16]{1,0:T(8,128)S(1)}, f32[128,16]{1,0:T(8,128)}, u32[]{:S(2)}) copy-start(f32[128,16]{1,0:T(8,128)} %copy.42) | copy-start | bytes 24580
  598.8 5.0 collective-permute-start
  603.9 5.8 collective-permute-start
  609.7 5.9 collective-permute-start
  615.6 5.8 collective-permute-start
  621.5 5.8 collective-permute-start
  627.3 7.2 collective-permute-start
  634.5 8.1 collective-permute-start
  642.6 8.1 collective-permute-start
  650.7 7.9 collective-permute-start
  658.6 7.9 collective-permute-start
  666.6 8.0 collective-permute-start
  674.6 7.8 collective-permute-start
  682.5 7.9 collective-permute-start
  690.4 8.1 collective-permute-start
  698.5 7.9 collective-permute-start
  706.5 14.1 %copy-start.19 = (f32[128,2,1024]{2,0,1:T(8,128)S(1)}, f32[128,2,1024]{2,0,1:T(8,128)}, u32[]{:S(2)}) copy-start(f32[128,2,1024]{2,0,1:T(8,128)} %copy-done.18) | copy-start | bytes 3145732
  706.5 14.1 %copy-start.24 = (bf16[128,1024]{1,0:T(8,128)(2,1)S(1)}, bf16[128,1024]{1,0:T(8,128)(2,1)}, u32[]{:S(2)}) copy-start(bf16[128,1024]{1,0:T(8,128)(2,1)} %copy-done.23) | copy-start | bytes 786436
  706.5 14.1 %copy-start.44 = (f32[1024]{0:T(1024)S(1)}, f32[1024]{0:T(1024)}, u32[]{:S(2)}) copy-start(f32[1024]{0:T(1024)} %param.28) | copy-start | bytes 12292
  720.5 46.3 %copy-start.21 = (bf16[16,4096]{1,0:T(8,128)(2,1)S(1)}, bf16[16,4096]{1,0:T(8,128)(2,1)}, u32[]{:S(2)}) copy-start(bf16[16,4096]{1,0:T(8,128)(2,1)} %param.19) | copy-start | bytes 393220
  720.5 47.3 %copy-start.38 = (f32[4096]{0:T(1024)S(1)}, f32[4096]{0:T(1024)}, u32[]{:S(2)}) copy-start(f32[4096]{0:T(1024)} %param.30) | copy-start | bytes 49156
  726.3 90.2 %all-gather.11.cloned.1.call-start = ((), (), s32[]{:S(2)}) async-start(), calls=%async_computation.9 | async-start | bytes 4718592 | tf_op jit(solution)/shard_map/all_gather | solution.py:116
  787.1 94.2 %reduce-scatter.5.cloned.1.call-start = ((), (), s32[]{:S(2)}) async-start(), calls=%async_computation.10 | async-start | bytes 4718592 | tf_op jit(solution)/shard_map/reduce_scatter | solution.py:122
  826.6 75.1 %copy-start.1 = (bf16[1024,288]{0,1:T(8,128)(2,1)S(1)}, bf16[1024,288]{0,1:T(8,128)(2,1)}, u32[]{:S(2)}) copy-start(bf16[1024,288]{0,1:T(8,128)(2,1)} %param.24) | copy-start | bytes 1769476
  843.2 47.2 %copy-start.41 = (f32[16,2]{0,1:T(2,128)S(1)}, f32[16,2]{0,1:T(2,128)}, u32[]{:S(2)}) copy-start(f32[16,2]{0,1:T(2,128)} %param.32) | copy-start | bytes 388
  843.2 57.4 %copy-start.22 = (bf16[16,4096]{1,0:T(8,128)(2,1)S(1)}, bf16[16,4096]{1,0:T(8,128)(2,1)}, u32[]{:S(2)}) copy-start(bf16[16,4096]{1,0:T(8,128)(2,1)} %reduce-scatter.3.cloned.1.call-done) | copy-start | bytes 393220
  883.3 17.2 %all-to-all-start.1 = ((bf16[16,4,4096]{2,1,0:T(4,128)(2,1)}), bf16[16,4,4096]{2,1,0:T(4,128)(2,1)S(1)}, u32[]{:S(2)}, u32[]{:S(2)}) async-start(bf16[16,4,4096]{2,1,0:T(4,128)(2,1)} %reshape.81), calls=%async_computation.3 | async-start | bytes 1048576 | tf_op jit(solution)/shard_map/all_to_all | solution.py:128
  (21 other events, 86.6 us)
Sparse Core Ops, SparseCore 0:
  9.1 25.7 all-gather.4
  37.0 111.3 all-gather.6
  163.4 60.1 all-reduce.29
  225.7 77.5 all-gather.8
  726.4 40.3 reduce-scatter.2
  787.2 29.2 all-gather.10
  843.4 37.8 reduce-scatter.4
where the time goes:
time: 924 us; the launch traced here: 909 us
  waiting for transfers between devices  327 us (35%)
  local copies, waits for them, and re-layouts  289 us (31%)
  other arithmetic  109 us (12%)
  starting transfers between devices  94.2 us (10%)
  matrix products  44.8 us (5%)
  blocking collectives  30.9 us (3%)
  between operations  14 us (2%)
    pad x24, local copies, waits for them, and re-layouts, per_device(): lax.associative_scan(combine_states, (decay, source), axis=0)  267 us
    all_gather x1, waiting for transfers between devices, per_device(): lax.all_gather(in_weight, 'seq', axis=1, tiled=True)  112 us
    ppermute x16, starting transfers between devices, from_behind(): return lax.ppermute(block, axis, route)  86.9 us
    psum x1, waiting for transfers between devices, per_device(): lax.psum(partial_value[:, :RANK].astype(jnp.bfloat16), 'expert')  44.8 us
    reduce_scatter x1, waiting for transfers between devices, per_device(): lax.psum_scatter(terms.astype(jnp.bfloat16), 'expert', scatter_dimension=...  39.7 us
    reduce_scatter x1, waiting for transfers between devices, per_device(): lax.psum_scatter(jnp.dot(act, w_down[0], preferred_element_type=jnp.float...  38 us
    add x12, other arithmetic, combine_states(): return (earlier[0] * later[0], later[0] * earlier[1] + later[1])  34.6 us
    add x12, other arithmetic, per_device(): lax.associative_scan(combine_states, (decay, source), axis=0)  33.2 us
  transfers between devices with their start and end apart: 24, of which 23 were waited for; matrix products, arithmetic and copies ran while one was open for 42% of the time, Pallas kernels for 0%

commit v1 on v0

--- a/solution.py
+++ b/solution.py
@@ -7,6 +7,11 @@
 CONV = 4
 RANK = 256
 TOP = 2
+
+
+def launch_the_ends(panel):
+    plain = jnp.sum(lax.all_gather(panel, "expert"), 0)
+    return plain
 
 
 def from_behind(block, axis, distance):
@@ -65,7 +70,7 @@
     inner = jax.nn.silu(conv).astype(jnp.bfloat16)
     partial_value = jnp.dot(inner, xproj_weight, preferred_element_type=jnp.float32)
     low_part, edge_part = (
-        lax.psum(partial_value[:, :RANK].astype(jnp.bfloat16), "expert").astype(jnp.float32),
+        launch_the_ends(partial_value[:, :RANK].astype(jnp.bfloat16)).astype(jnp.float32),
         lax.psum(partial_value[:, RANK:].astype(jnp.bfloat16), "expert").astype(jnp.float32),
     )
     dt_low = low_part.astype(jnp.bfloat16)

time: 924 us -> 894 us (0.968)
  waiting for transfers between devices: 327 us -> 282 us
  blocking collectives: 30.9 us -> 44.3 us
    psum x1 -> x0, waiting for transfers between devices: 44.8 us -> none  [per_device(): lax.psum(partial_value[:, :RANK].astype(jnp.bfloat16), 'expert')]
    all_gather x0 -> x1, blocking collectives: none -> 12.9 us  [launch_the_ends(): plain = jnp.sum(lax.all_gather(panel, 'expert'), 0)]
  transfers between devices with their start and end apart: 24 -> 23, of which waited for: 23 -> 22; matrix products, arithmetic and copies ran while one was open for 42% -> 45% of each run, Pallas kernels for 0% -> 0%
where the time goes in v1:
time: 894 us; the launch traced here: 878 us
  local copies, waits for them, and re-layouts  287 us (32%)
  waiting for transfers between devices  282 us (32%)
  other arithmetic  110 us (12%)
  starting transfers between devices  96.7 us (11%)
  blocking collectives  44.3 us (5%)
  matrix products  44.1 us (5%)
  between operations  14 us (2%)
    pad x24, local copies, waits for them, and re-layouts, per_device(): lax.associative_scan(combine_states, (decay, source), axis=0)  266 us
    all_gather x1, waiting for transfers between devices, per_device(): lax.all_gather(in_weight, 'seq', axis=1, tiled=True)  112 us
    ppermute x16, starting transfers between devices, from_behind(): return lax.ppermute(block, axis, route)  89.4 us
    reduce_scatter x1, waiting for transfers between devices, per_device(): lax.psum_scatter(terms.astype(jnp.bfloat16), 'expert', scatter_dimension=...  39.9 us
    reduce_scatter x1, waiting for transfers between devices, per_device(): lax.psum_scatter(jnp.dot(act, w_down[0], preferred_element_type=jnp.float...  37.9 us
    add x12, other arithmetic, combine_states(): return (earlier[0] * later[0], later[0] * earlier[1] + later[1])  34.5 us
    add x12, other arithmetic, per_device(): lax.associative_scan(combine_states, (decay, source), axis=0)  33.2 us
    all_gather x1, waiting for transfers between devices, per_device(): lax.all_gather(received.reshape(1, slots_all, dim), 'expert', axis=0, til...  29.3 us
  transfers between devices with their start and end apart: 23, of which 22 were waited for; matrix products, arithmetic and copies ran while one was open for 45% of the time, Pallas kernels for 0%

profile of v1, /device:TPU:0, one launch (start us, length us, event | category | flops | bytes accessed | tf_op | source)
XLA Modules:
  0.0 878.2 jit_solution(4939895551040621163)
XLA Ops:
  9.7 25.2 %all-gather.6.cloned.1.call-done = bf16[128,4096]{1,0:T(8,128)(2,1)} async-done(((bf16[16,4096]{1,0:T(8,128)(2,1)}), bf16[128,4096]{1,0:T(8,128)(2,1)}) %all-gather.6.cloned.1.call-update) | async-done | bytes 1048592 | tf_op jit(solution)/shard_map/all_gather | solution.py:54
  36.4 112.0 %all-gather.8.cloned.1.call-done = bf16[2,4096,1024]{2,1,0:T(8,128)(2,1)} async-done(((bf16[2,256,1024]{2,1,0:T(8,128)(2,1)}), bf16[2,4096,1024]{2,1,0:T(8,128)(2,1)}) %all-gather.8.cloned.1.call-update) | async-done | bytes 16777232 | tf_op jit(solution)/shard_map/all_gather | solution.py:60
  148.4 8.5 fusion.20
  162.6 12.9 %all-gather = bf16[1024,256]{0,1:T(8,128)(2,1)S(1)} all-gather(bf16[128,256]{0,1:T(8,128)(2,1)S(1)} %slice.344), channel_id=2, replica_groups=mesh['seq'=16,'expert'=8] {'expert'}, dimensions={0}, use_global_device_ids=true | all-gather | bytes 589824 | tf_op jit(solution)/shard_map/all_gather | solution.py:13
  175.7 14.4 %psum.7 = bf16[128,32]{0,1:T(8,128)(2,1)S(1)} all-reduce(bf16[128,32]{0,1:T(8,128)(2,1)S(1)} %slice.341), channel_id=1, replica_groups=mesh['seq'=16,'expert'=8] {'expert'}, use_global_device_ids=true, to_apply=%region_1.2 | all-reduce | flops 4096 | bytes 16384 | tf_op jit(solution)/shard_map/psum | solution.py:74
  199.6 10.9 %slice_add_fusion = (f32[64,16,1024]{2,1,0:T(8,128)S(1)}, f32[64,16,1024]{2,1,0:T(8,128)}) fusion(f32[128,16,1024]{2,1,0:T(8,128)} %copy-done.3, f32[128,16,1024]{2,1,0:T(8,128)} %copy-done.2), kind=kLoop, calls=%fused_computation.19 | loop fusion | flops 3145728 | bytes 25165824 | tf_op jit(solution)/shard_map/add | solution.py:29
  275.0 7.0 pad.108
  282.0 10.2 %pad.109 = f32[32,16,1024]{2,1,0:T(8,128)} pad(f32[16,16,1024]{2,1,0:T(8,128)} %add.261, f32[]{:T(128)} %constant.15.clone.1), padding=1_0_1x0_0_0x0_0_0 | pad | bytes 3145732 | tf_op jit(solution)/shard_map/pad | solution.py:83
  292.2 10.1 %pad.95 = f32[32,16,1024]{2,1,0:T(8,128)} pad(f32[16,16,1024]{2,1,0:T(8,128)} %add.251, f32[]{:T(128)} %constant.15.clone.1), padding=1_0_1x0_0_0x0_0_0 | pad | bytes 3145732 | tf_op jit(solution)/shard_map/pad | solution.py:83
  304.6 10.1 %pad.94 = f32[32,16,1024]{2,1,0:T(8,128)} pad(f32[16,16,1024]{2,1,0:T(8,128)} %pad_maximum_fusion.4, f32[]{:T(128)} %constant.15.clone.1), padding=0_1_1x0_0_0x0_0_0 | pad | bytes 3145732 | tf_op jit(solution)/shard_map/pad | solution.py:83
  322.0 5.0 fusion.16
  328.7 18.6 %pad.96 = f32[64,16,1024]{2,1,0:T(8,128)} pad(f32[32,16,1024]{2,1,0:T(8,128)} %pad_maximum_fusion.2, f32[]{:T(128)} %constant.15.clone.1), padding=0_1_1x0_0_0x0_0_0 | pad | bytes 6291460 | tf_op jit(solution)/shard_map/pad | solution.py:83
  347.2 12.0 %pad.97 = f32[64,16,1024]{2,1,0:T(8,128)} pad(f32[32,16,1024]{2,1,0:T(8,128)S(1)} %copy-done.16, f32[]{:T(128)} %constant.15.clone.1), padding=1_0_1x0_0_0x0_0_0 | pad | bytes 6291460 | tf_op jit(solution)/shard_map/pad | solution.py:83
  359.2 6.8 add.255
  366.0 35.6 %pad.99 = f32[128,16,1024]{2,1,0:T(8,128)} pad(f32[64,16,1024]{2,1,0:T(8,128)} %add.255, f32[]{:T(128)} %constant.15.clone.1), padding=1_0_1x0_0_0x0_0_0 | pad | bytes 12582916 | tf_op jit(solution)/shard_map/pad | solution.py:83
  403.1 18.6 %pad.110 = f32[64,16,1024]{2,1,0:T(8,128)} pad(f32[32,16,1024]{2,1,0:T(8,128)} %pad_maximum_fusion.3, f32[]{:T(128)} %constant.15.clone.1), padding=0_1_1x0_0_0x0_0_0 | pad | bytes 6291460 | tf_op jit(solution)/shard_map/pad | solution.py:83
  421.7 12.0 %pad.111 = f32[64,16,1024]{2,1,0:T(8,128)} pad(f32[32,16,1024]{2,1,0:T(8,128)S(1)} %copy-done.15, f32[]{:T(128)} %constant.15.clone.1), padding=1_0_1x0_0_0x0_0_0 | pad | bytes 6291460 | tf_op jit(solution)/shard_map/pad | solution.py:83
  433.7 7.1 add.263
  442.3 7.5 fusion.12
  452.4 35.6 %pad.98 = f32[128,16,1024]{2,1,0:T(8,128)} pad(f32[64,16,1024]{2,1,0:T(8,128)} %pad_maximum_fusion, f32[]{:T(128)} %constant.15.clone.1), padding=0_1_1x0_0_0x0_0_0 | pad | bytes 12582916 | tf_op jit(solution)/shard_map/pad | solution.py:83
  488.0 35.5 %pad.113 = f32[128,16,1024]{2,1,0:T(8,128)} pad(f32[64,16,1024]{2,1,0:T(8,128)} %add.263, f32[]{:T(128)} %constant.15.clone.1), padding=1_0_1x0_0_0x0_0_0 | pad | bytes 12582916 | tf_op jit(solution)/shard_map/pad | solution.py:83
  523.5 4.7 pad_maximum_fusion.1
  528.3 35.4 %pad.112 = f32[128,16,1024]{2,1,0:T(8,128)} pad(f32[64,16,1024]{2,1,0:T(8,128)} %pad_maximum_fusion.1, f32[]{:T(128)} %constant.15.clone.1), padding=0_1_1x0_0_0x0_0_0 | pad | bytes 12582916 | tf_op jit(solution)/shard_map/pad | solution.py:83
  565.6 110.3 %while.11 = (s32[]{:T(128)}, f32[16,1024]{1,0:T(8,128)S(1)}, f32[16,1024]{1,0:T(8,128)S(1)}, f32[16,1024]{1,0:T(8,128)S(1)}, s32[]{:T(128)}, /*index=5*/s32[]{:T(128)}) while((s32[]{:T(128)}, f32[16,1024]{1,0:T(8,128)S(1)}, f32[16,1024]{1,0:T(8,128)S(1)}, f32[16,1024]{1,0:T(8,128)S(1)}, s32[]{:T(128)}, /*index=5*/s32[]{:T(128)}) %tuple.47), condition=%wide.region_4.5_spmd.clone, body=%wide.region_3.4_spmd.clone.sunk | while | flops 81923 | bytes 458871 | solution.py:92
  565.6 4.5 collective-permute-start
  577.5 4.3 collective-permute-start
  583.6 4.4 collective-permute-start
  589.5 5.3 collective-permute-start
  596.4 6.3 collective-permute-start
  604.4 6.5 collective-permute-start
  612.4 6.2 collective-permute-start
  620.3 6.3 collective-permute-start
  628.2 6.3 collective-permute-start
  636.1 6.3 collective-permute-start
  644.1 6.4 collective-permute-start
  652.1 6.3 collective-permute-start
  660.0 6.3 collective-permute-start
  667.9 6.3 collective-permute-start
  675.9 14.0 %multiply_reduce_fusion = f32[128,1024]{1,0:T(8,128)S(1)} fusion(f32[128,16,1024]{2,1,0:T(8,128)} %pad.112, f32[128,16,1024]{2,1,0:T(8,128)} %pad.113, f32[128,16,1024]{2,1,0:T(8,128)} %pad.98, f32[128,16,1024]{2,1,0:T(8,128)} %pad.99, f32[16,1024]{1,0:T(8,128)S(1)} %get-tuple-element.27, f32[128,16]{1,0:T(8,128)S(1)} %copy.42), kind=kLoop, calls=%fused_computation.3 | loop fusion | flops 12451840 | bytes 34152448 | tf_op jit(solution)/shard_map/reduce_sum | solution.py:94
  689.9 5.7 convolution_convert_fusion
  696.5 39.9 %reduce-scatter.3.cloned.1.call-done = bf16[16,4096]{1,0:T(8,128)(2,1)} async-done(((bf16[128,4096]{1,0:T(8,128)(2,1)}), bf16[16,4096]{1,0:T(8,128)(2,1)}) %reduce-scatter.3.cloned.1.call-update) | async-done | bytes 131088 | tf_op jit(solution)/shard_map/reduce_scatter | solution.py:101
  738.9 16.9 %all_to_all.10 = bf16[16,4,4096]{2,1,0:T(4,128)(2,1)S(1)} all-to-all(bf16[16,4,4096]{2,1,0:T(4,128)(2,1)S(1)} %reshape.78), channel_id=1, replica_groups=mesh['seq'=16,'expert'=8] {'seq'}, dimensions={0} | all-to-all | bytes 1048576 | tf_op jit(solution)/shard_map/all_to_all | solution.py:118
  756.8 29.3 %all-gather.12.cloned.1.call-done = bf16[8,64,4096]{2,1,0:T(8,128)(2,1)} async-done(((bf16[1,64,4096]{2,1,0:T(8,128)(2,1)}), bf16[8,64,4096]{2,1,0:T(8,128)(2,1)}) %all-gather.12.cloned.1.call-update) | async-done | bytes 4194320 | tf_op jit(solution)/shard_map/all_gather | solution.py:121
  786.2 10.1 %fusion.6 = f32[512,896]{1,0:T(8,128)} fusion(bf16[512,4096]{1,0:T(8,128)(2,1)} %bitcast.57, bf16[1,4096,896]{2,1,0:T(8,128)(2,1)} %param.33), kind=kOutput, calls=%fused_computation.9 | convolution fusion | flops 3758096384 | bytes 13369344 | tf_op jit(solution)/shard_map/dot_general | solution.py:124
  796.2 16.7 %fusion.8 = bf16[512,4096]{1,0:T(8,128)(2,1)} fusion(bf16[1,896,4096]{2,1,0:T(8,128)(2,1)} %param.35, f32[512,896]{1,0:T(8,128)} %fusion.6, bf16[512,4096]{1,0:T(8,128)(2,1)} %bitcast.58, bf16[1,4096,896]{2,1,0:T(8,128)(2,1)} %param.34), kind=kOutput, calls=%fused_computation.11 | convolution fusion | flops 7521042432 | bytes 24903680 | tf_op jit(solution)/shard_map/dot_general | solution.py:128
  812.9 37.9 %reduce-scatter.5.cloned.1.call-done = bf16[64,4096]{1,0:T(8,128)(2,1)} async-done(((bf16[512,4096]{1,0:T(8,128)(2,1)}), bf16[64,4096]{1,0:T(8,128)(2,1)}) %reduce-scatter.5.cloned.1.call-update) | async-done | bytes 524304 | tf_op jit(solution)/shard_map/reduce_scatter | solution.py:127
  852.9 7.1 all-to-all-start.1
  860.1 10.1 %all-to-all-done.1 = bf16[16,4,4096]{2,1,0:T(4,128)(2,1)S(1)} async-done(((bf16[16,4,4096]{2,1,0:T(4,128)(2,1)}), bf16[16,4,4096]{2,1,0:T(4,128)(2,1)S(1)}, u32[]{:S(2)}, u32[]{:S(2)}) %all-to-all-start.1) | async-done | bytes 524320 | tf_op jit(solution)/shard_map/all_to_all | solution.py:133
  (239 shorter events, 138.8 us)
Async XLA Ops:
  6.5 155.7 %copy-start = (bf16[1024,288]{0,1:T(8,128)(2,1)S(1)}, bf16[1024,288]{0,1:T(8,128)(2,1)}, u32[]{:S(2)}) copy-start(bf16[1024,288]{0,1:T(8,128)(2,1)} %param.24) | copy-start | bytes 1769476
  6.5 28.4 %all-gather.6.cloned.1.call-start = ((), (), s32[]{:S(2)}) async-start(), calls=%async_computation.4 | async-start | bytes 1179648 | tf_op jit(solution)/shard_map/all_gather | solution.py:54
  7.3 141.1 %all-gather.8.cloned.1.call-start = ((), (), s32[]{:S(2)}) async-start(), calls=%async_computation.5 | async-start | bytes 17825792 | tf_op jit(solution)/shard_map/all_gather | solution.py:60
  8.0 681.9 %all-gather.10.cloned.1.call-start = ((), (), s32[]{:S(2)}) async-start(), calls=%async_computation.6 | async-start | bytes 8912896 | tf_op jit(solution)/shard_map/all_gather | solution.py:98
  8.7 727.6 %reduce-scatter.3.cloned.1.call-start = ((), (), s32[]{:S(2)}) async-start(), calls=%async_computation.7 | async-start | bytes 1179648 | tf_op jit(solution)/shard_map/reduce_scatter | solution.py:101
  36.4 125.5 %copy-start.38 = (f32[1024]{0:T(1024)S(1)}, f32[1024]{0:T(1024)}, u32[]{:S(2)}) copy-start(f32[1024]{0:T(1024)} %param.23) | copy-start | bytes 12292
  156.9 33.7 %copy-start.41 = (bf16[256,1024]{1,0:T(8,128)(2,1)S(1)}, bf16[256,1024]{1,0:T(8,128)(2,1)}, u32[]{:S(2)}) copy-start(bf16[256,1024]{1,0:T(8,128)(2,1)} %param.25) | copy-start | bytes 1572868
  156.9 33.7 %copy-start.42 = (f32[1024]{0:T(1024)S(1)}, f32[1024]{0:T(1024)}, u32[]{:S(2)}) copy-start(f32[1024]{0:T(1024)} %param.26) | copy-start | bytes 12292
  156.9 34.2 %copy-start.36 = (f32[16,1024]{1,0:T(8,128)S(1)}, f32[16,1024]{1,0:T(8,128)}, u32[]{:S(2)}) copy-start(f32[16,1024]{1,0:T(8,128)} %param.27) | copy-start | bytes 196612
  156.9 5.0 collective-permute-start.1
  162.3 30.9 %copy-start.23 = (bf16[128,1024]{1,0:T(8,128)(2,1)}, bf16[128,1024]{1,0:T(8,128)(2,1)S(1)}, u32[]{:S(2)}) copy-start(bf16[128,1024]{1,0:T(8,128)(2,1)S(1)} %multiply_convert_fusion.1) | copy-start | bytes 786436
  232.2 13.9 %copy-start.35 = (f32[1,16,1024]{2,1,0:T(8,128)S(1)}, f32[1,16,1024]{2,1,0:T(8,128)}, u32[]{:S(2)}) copy-start(f32[1,16,1024]{2,1,0:T(8,128)} %slice.349) | copy-start | bytes 196612
  254.3 9.1 %copy-start.20 = (f32[8,16,1024]{2,1,0:T(8,128)S(1)}, f32[8,16,1024]{2,1,0:T(8,128)}, u32[]{:S(2)}) copy-start(f32[8,16,1024]{2,1,0:T(8,128)} %add.249) | copy-start | bytes 1572868
  275.0 27.3 %copy-start.32 = (f32[1,16,1024]{2,1,0:T(8,128)S(1)}, f32[1,16,1024]{2,1,0:T(8,128)}, u32[]{:S(2)}) copy-start(f32[1,16,1024]{2,1,0:T(8,128)} %slice.347) | copy-start | bytes 196612
  328.7 18.6 %copy-start.16 = (f32[32,16,1024]{2,1,0:T(8,128)S(1)}, f32[32,16,1024]{2,1,0:T(8,128)}, u32[]{:S(2)}) copy-start(f32[32,16,1024]{2,1,0:T(8,128)} %add.253) | copy-start | bytes 6291460
  366.0 35.6 %copy-start.17 = (f32[31,16,1024]{2,1,0:T(8,128)S(1)}, f32[31,16,1024]{2,1,0:T(8,128)}, u32[]{:S(2)}) copy-start(f32[31,16,1024]{2,1,0:T(8,128)} %get-tuple-element.56) | copy-start | bytes 6094852
  366.0 35.6 %copy-start.30 = (f32[1,16,1024]{2,1,0:T(8,128)S(1)}, f32[1,16,1024]{2,1,0:T(8,128)}, u32[]{:S(2)}) copy-start(f32[1,16,1024]{2,1,0:T(8,128)} %slice.369) | copy-start | bytes 196612
  403.1 18.6 %copy-start.15 = (f32[32,16,1024]{2,1,0:T(8,128)S(1)}, f32[32,16,1024]{2,1,0:T(8,128)}, u32[]{:S(2)}) copy-start(f32[32,16,1024]{2,1,0:T(8,128)} %add.262) | copy-start | bytes 6291460
  433.7 7.1 copy-start.5
  433.7 8.6 copy-start.6
  442.3 7.6 copy-start.29
  488.0 35.5 %copy-start.28 = (f32[1,16,1024]{2,1,0:T(8,128)S(1)}, f32[1,16,1024]{2,1,0:T(8,128)}, u32[]{:S(2)}) copy-start(f32[1,16,1024]{2,1,0:T(8,128)} %slice.368) | copy-start | bytes 196612
  565.6 6.1 collective-permute-start
  571.7 5.8 collective-permute-start
  577.5 6.0 collective-permute-start
  583.6 5.9 collective-permute-start
  589.5 6.9 collective-permute-start
  596.4 7.9 collective-permute-start
  604.4 8.0 collective-permute-start
  612.4 7.8 collective-permute-start
  620.3 7.9 collective-permute-start
  628.2 7.9 collective-permute-start
  636.1 7.9 collective-permute-start
  644.1 8.0 collective-permute-start
  652.1 7.9 collective-permute-start
  660.0 7.9 collective-permute-start
  667.9 7.9 collective-permute-start
  675.8 14.1 %copy-start.19 = (f32[128,2,1024]{2,0,1:T(8,128)S(1)}, f32[128,2,1024]{2,0,1:T(8,128)}, u32[]{:S(2)}) copy-start(f32[128,2,1024]{2,0,1:T(8,128)} %copy-done.18) | copy-start | bytes 3145732
  675.8 14.1 %copy-start.24 = (bf16[128,1024]{1,0:T(8,128)(2,1)S(1)}, bf16[128,1024]{1,0:T(8,128)(2,1)}, u32[]{:S(2)}) copy-start(bf16[128,1024]{1,0:T(8,128)(2,1)} %copy-done.23) | copy-start | bytes 786436
  675.9 14.1 %copy-start.43 = (f32[1024]{0:T(1024)S(1)}, f32[1024]{0:T(1024)}, u32[]{:S(2)}) copy-start(f32[1024]{0:T(1024)} %param.28) | copy-start | bytes 12292
  689.8 46.5 %copy-start.21 = (bf16[16,4096]{1,0:T(8,128)(2,1)S(1)}, bf16[16,4096]{1,0:T(8,128)(2,1)}, u32[]{:S(2)}) copy-start(bf16[16,4096]{1,0:T(8,128)(2,1)} %param.19) | copy-start | bytes 393220
  689.9 47.6 %copy-start.37 = (f32[4096]{0:T(1024)S(1)}, f32[4096]{0:T(1024)}, u32[]{:S(2)}) copy-start(f32[4096]{0:T(1024)} %param.30) | copy-start | bytes 49156
  695.7 90.5 %all-gather.12.cloned.1.call-start = ((), (), s32[]{:S(2)}) async-start(), calls=%async_computation.8 | async-start | bytes 4718592 | tf_op jit(solution)/shard_map/all_gather | solution.py:121
  756.8 94.1 %reduce-scatter.5.cloned.1.call-start = ((), (), s32[]{:S(2)}) async-start(), calls=%async_computation.9 | async-start | bytes 4718592 | tf_op jit(solution)/shard_map/reduce_scatter | solution.py:127
  796.2 75.1 %copy-start.1 = (bf16[1024,288]{0,1:T(8,128)(2,1)S(1)}, bf16[1024,288]{0,1:T(8,128)(2,1)}, u32[]{:S(2)}) copy-start(bf16[1024,288]{0,1:T(8,128)(2,1)} %param.24) | copy-start | bytes 1769476
  812.9 47.1 %copy-start.40 = (f32[16,2]{0,1:T(2,128)S(1)}, f32[16,2]{0,1:T(2,128)}, u32[]{:S(2)}) copy-start(f32[16,2]{0,1:T(2,128)} %param.32) | copy-start | bytes 388
  812.9 57.4 %copy-start.22 = (bf16[16,4096]{1,0:T(8,128)(2,1)S(1)}, bf16[16,4096]{1,0:T(8,128)(2,1)}, u32[]{:S(2)}) copy-start(bf16[16,4096]{1,0:T(8,128)(2,1)} %reduce-scatter.3.cloned.1.call-done) | copy-start | bytes 393220
  852.9 17.3 %all-to-all-start.1 = ((bf16[16,4,4096]{2,1,0:T(4,128)(2,1)}), bf16[16,4,4096]{2,1,0:T(4,128)(2,1)S(1)}, u32[]{:S(2)}, u32[]{:S(2)}) async-start(bf16[16,4,4096]{2,1,0:T(4,128)(2,1)} %reshape.81), calls=%async_computation.3 | async-start | bytes 1048576 | tf_op jit(solution)/shard_map/all_to_all | solution.py:133
  (19 other events, 72.6 us)
Sparse Core Ops, SparseCore 0:
  9.1 25.7 all-gather.5
  37.0 111.3 all-gather.7
  150.5 78.3 all-gather.9
  695.8 40.5 reduce-scatter.2
  756.9 29.1 all-gather.11
  813.1 37.7 reduce-scatter.4
